TPU v7x, 32 devices: a whole 2x2x4 slice. The times are simulated.
32 devices in a mesh: fsdp: 4 (over z), seq: 2 (over x), head: 4 (over y, core).
Axes of the slice: x: 2, y: 2, z: 4, core: 2. Of those that a mesh axis runs over, the one named last changes fastest.
Arguments:
- queries: bfloat16 [2048, 4096], P(('fsdp', 'seq'), 'head'), may hold values from -6 to 6
- span_k: bfloat16 [2048, 512], P(('fsdp', 'seq'), 'head'), may hold values from -6 to 6
- span_v: bfloat16 [2048, 512], P(('fsdp', 'seq'), 'head'), may hold values from -6 to 6
- cache_k: bfloat16 [512, 128, 512], P(('fsdp', 'seq'), None, 'head'), may hold values from -6 to 6
- cache_v: bfloat16 [512, 128, 512], P(('fsdp', 'seq'), None, 'head'), may hold values from -6 to 6
- block_slot: int32 [512], replicated, may hold values from 0 to 511, as said below
- pattern: int32 [16, 48], P(('fsdp', 'seq')), may hold values from 0 to 511, as said below
- wo: bfloat16 [4096, 8192], P('head', 'fsdp'), may hold values from -6 to 6
Outputs:
- mixed: bfloat16 [2048, 8192], P(('fsdp', 'seq'))
Inputs may be any that keep to these rules, and one draw needn't show every extreme that they name: `pattern`: each row lists 48 different blocks. Of the 96 entries in the rows of one index of fsdp and seq, all are different, at most 24 have a storage row block_slot between o * 64 and (o + 1) * 64 - 1 for any o, and exactly 24 do for some o. A permutation: block c is stored at row block_slot[c] of cache_k and cache_v.
All inputs are finite; a program needn't handle non-finite values.
Results may differ from a plain program's by a relative error of at most 0.0095.
Values may be sent and summed in bfloat16 or wider, within the bound.
No kernel may reach another device: no remote copies, remote signals or barrier semaphores. Data moves between devices by JAX's collectives and lax.ppermute only.
A program may use at most 128 MiB of HBM per device.

v0:
```python
import jax
import jax.numpy as jnp
from jax import lax
from jax.sharding import PartitionSpec as P

HD = 128


def from_behind(value, axis, steps):
    count = lax.axis_size(axis)
    leading, last = (max(0, -steps), min(count, count - steps))
    return lax.ppermute(value, axis, [(source, source + steps) for source in range(leading, last)])


def attend_block(query_block, keys, values, present):
    length = keys.shape[0]
    block_len = query_block.shape[0]
    kv_local = query_block.shape[1]
    head_dim = query_block.shape[3]
    keys_four = keys.reshape(length, kv_local, head_dim)
    values_four = values.reshape(length, kv_local, head_dim)
    scores = jnp.einsum(
        "tkgd,lkd->kgtl", query_block, keys_four, preferred_element_type=jnp.float32
    ) / jnp.sqrt(jnp.float32(head_dim))
    column = jnp.arange(length)[None, :]
    row_ids = jnp.arange(block_len)[:, None]
    listed_end = length - 2 * block_len
    own_start = listed_end + block_len
    allowed = (
        (column < listed_end)
        | (column >= listed_end) & (column < own_start) & present
        | (column >= own_start) & (column - own_start <= row_ids)
    )
    scores = jnp.where(allowed, scores, -jnp.inf)
    top = jnp.max(scores, axis=-1, keepdims=True)
    expo = jnp.exp(scores - top)
    probs_bf = (expo / jnp.sum(expo, axis=-1, keepdims=True)).astype(jnp.bfloat16)
    output = jnp.einsum("kgtl,lkd->tkgd", probs_bf, values_four, preferred_element_type=jnp.float32)
    return output.reshape(block_len, -1).astype(jnp.bfloat16)


def body(queries, span_k, span_v, cache_k, cache_v, block_slot, pattern, wo):
    seq_devs = lax.axis_size(("fsdp", "seq"))
    index_here = lax.axis_index(("fsdp", "seq"))
    qb_local, list_len = pattern.shape
    cb_local, block_len, kv_cols = cache_k.shape
    kv_local = kv_cols // HD
    group_size = queries.shape[1] // kv_cols
    requests = qb_local * list_len
    capacity = max(2, 2 * requests // seq_devs)
    slot_ids = block_slot[pattern.reshape(-1)]
    owners = slot_ids // cb_local
    within = slot_ids % cb_local
    position = jnp.arange(requests)
    earlier = (owners[None, :] == owners[:, None]) & (position[None, :] < position[:, None])
    ranking = jnp.sum(earlier.astype(jnp.int32), axis=1)
    places = owners * capacity + ranking
    wanted = jnp.zeros((seq_devs * capacity,), jnp.int32).at[places].set(within)
    asked_ids = lax.all_to_all(
        wanted.reshape(seq_devs, capacity), ("fsdp", "seq"), split_axis=0, concat_axis=0, tiled=True
    ).reshape(-1)
    send_k = cache_k[asked_ids]
    send_v = cache_v[asked_ids]
    got_k, got_v = (
        lax.all_to_all(send_k, ("fsdp", "seq"), split_axis=0, concat_axis=0, tiled=True),
        lax.all_to_all(send_v, ("fsdp", "seq"), split_axis=0, concat_axis=0, tiled=True),
    )
    listed_k = got_k[places].reshape(qb_local, list_len * block_len, kv_cols)
    listed_v = got_v[places].reshape(qb_local, list_len * block_len, kv_cols)
    prev_k, prev_v = from_behind((span_k[-block_len:], span_v[-block_len:]), ("fsdp", "seq"), 1)
    own_k = span_k.reshape(qb_local, block_len, kv_cols)
    own_v = span_v.reshape(qb_local, block_len, kv_cols)
    before_k = jnp.concatenate([prev_k[None], own_k[:-1]], axis=0)
    before_v = jnp.concatenate([prev_v[None], own_v[:-1]], axis=0)
    present = index_here * qb_local + jnp.arange(qb_local) > 0
    query_blocks = queries.reshape(qb_local, block_len, kv_local, group_size, HD)

    def one_block(inputs):
        query_block, list_keys, list_values, prior_k, prior_v, self_k, self_v, flag = inputs
        keys = jnp.concatenate([list_keys, prior_k, self_k], axis=0)
        values = jnp.concatenate([list_values, prior_v, self_v], axis=0)
        return attend_block(query_block, keys, values, flag)

    attended = lax.map(
        one_block, (query_blocks, listed_k, listed_v, before_k, before_v, own_k, own_v, present)
    )
    attended = attended.reshape(qb_local * block_len, -1)
    partial_terms = jnp.dot(
        lax.all_gather(attended, "fsdp", axis=0, tiled=True), wo, preferred_element_type=jnp.float32
    )
    summed = lax.psum(partial_terms.astype(jnp.bfloat16), "head")
    mixed = lax.all_to_all(summed, "fsdp", split_axis=0, concat_axis=1, tiled=True)
    return mixed


def solution(mesh):
    return jax.shard_map(
        body,
        mesh=mesh,
        in_specs=(
            P(("fsdp", "seq"), "head"),
            P(("fsdp", "seq"), "head"),
            P(("fsdp", "seq"), "head"),
            P(("fsdp", "seq"), None, "head"),
            P(("fsdp", "seq"), None, "head"),
            P(),
            P(("fsdp", "seq"), None),
            P("head", "fsdp"),
        ),
        out_specs=P(("fsdp", "seq"), None),
        check_vma=False,
    )
```

profile of v0, /device:TPU:0, one launch (start us, length us, event | category | flops | bytes accessed | tf_op | source)
XLA Modules:
  0.0 671.5 jit_solution(15058258182614903326)
XLA Ops:
  6.5 0.9 reshape.261
  7.5 1.6 gather_fusion
  9.1 0.2 convert_reduce_fusion
  9.3 0.9 scatter_custom_fusion
  10.3 13.5 %all_to_all.38 = s32[8,1,24]{2,1,0:T(1,128)S(1)} all-to-all(s32[8,1,24]{2,1,0:T(1,128)S(1)} %all_to_all.26), channel_id=1, replica_groups=mesh['fsdp'=4,'seq'=2,'head'=4] {'fsdp','seq'}, dimensions={0} | all-to-all | bytes 1536 | tf_op jit(solution)/shard_map/all_to_all | solution.py:59
  23.8 0.5 broadcast.294
  24.3 0.7 reduce.11
  25.1 8.0 %gather_fusion.1 = bf16[192,128,128]{2,1,0:T(8,128)(2,1)} fusion(bf16[64,128,128]{2,1,0:T(8,128)(2,1)S(1)} %copy-done, s32[1024]{0:T(1024)S(1)} %pad_clamp_fusion.1), kind=kCustom, calls=%fused_computation.1 | custom fusion | bytes 12583680 | tf_op jit(solution)/shard_map/gather | solution.py:63
  33.1 4.9 all-to-all-start.1
  38.0 7.9 %gather_fusion.3 = bf16[192,128,128]{2,1,0:T(8,128)(2,1)} fusion(bf16[64,128,128]{2,1,0:T(8,128)(2,1)S(1)} %copy-done.3, s32[1024]{0:T(1024)S(1)} %pad_clamp_fusion.1), kind=kCustom, calls=%fused_computation.3 | custom fusion | bytes 12583680 | tf_op jit(solution)/shard_map/gather | solution.py:62
  45.9 129.0 %all-to-all-done.1 = bf16[192,128,128]{2,1,0:T(8,128)(2,1)} async-done(((bf16[192,128,128]{2,1,0:T(8,128)(2,1)}), bf16[192,128,128]{2,1,0:T(8,128)(2,1)}, u32[]{:S(2)}, u32[]{:S(2)}) %all-to-all-start.1) | async-done | bytes 6291488 | tf_op jit(solution)/shard_map/all_to_all | solution.py:66
  175.0 4.8 all-to-all-start.2
  179.9 3.8 collective-permute-start
  183.7 3.6 collective-permute-start.1
  187.5 43.7 %collective-permute-done = bf16[128,128]{0,1:T(8,128)(2,1)S(1)} collective-permute-done((bf16[128,128]{0,1:T(8,128)(2,1)S(1)}, bf16[128,128]{0,1:T(8,128)(2,1)S(1)}, u32[]{:S(2)}, u32[]{:S(2)}) %collective-permute-start) | collective-permute-done | bytes 32800 | tf_op jit(solution)/shard_map/ppermute | solution.py:12
  231.3 0.5 collective-permute-done.1
  231.7 5.5 gather_fusion.2
  237.2 79.8 %all-to-all-done.2 = bf16[192,128,128]{2,1,0:T(8,128)(2,1)} async-done(((bf16[192,128,128]{2,1,0:T(8,128)(2,1)}), bf16[192,128,128]{2,1,0:T(8,128)(2,1)}, u32[]{:S(2)}, u32[]{:S(2)}) %all-to-all-start.2) | async-done | bytes 6291488 | tf_op jit(solution)/shard_map/all_to_all | solution.py:65
  317.0 5.5 gather_fusion.4
  322.5 97.4 %while.12 = (s32[]{:T(128)}, bf16[2,128,1024]{2,1,0:T(8,128)(2,1)}, bf16[2,6144,128]{2,1,0:T(8,128)(2,1)}, bf16[2,128,128]{1,2,0:T(8,128)(2,1)S(1)}, bf16[2,128,...) while((s32[]{:T(128)}, bf16[2,128,1024]{2,1,0:T(8,128)(2,1)}, ...), condition=%wide.region_5.6_spmd, body=%wide.region_2.5_spmd.sunk | while | flops 3446554624 | bytes 113933528 | solution.py:84
  322.5 0.6 dynamic_slice.72
  323.1 0.6 iota_compare_fusion.7
  323.7 5.8 fusion.40
  329.5 1.5 dynamic-slice_bitcast_fusion.8
  331.1 13.2 %fusion.41 = (f32[8,128]{1,0:T(8,128)S(1)}, f32[6400,128,8]{1,0,2:T(8,128)}) fusion(pred[128,6400]{0,1:T(8,128)(4,1)S(1)} %fusion.40, bf16[1,128,1,8,128]{4,3,1,0,2:T(8,128)(2,1)S(1)} %constant_dynamic-slice_fusion.6, bf16[128,128]{1,0:T(8,128)(2,1)S(1)} %get-tuple-element.252, bf16[128,128]{1,0:T(8,128)(2,1)S(1)} %get-tuple-element.253, ...), kind=kOutput, calls=%fused_computation.10.clone.1 | convolution fusion | flops 1702296576 | bytes 28938240 | tf_op jit(solution)/shard_map/while/body/eval_jaxpr/tkgd,lkd->kgtl/dot_general | solution.py:22
  344.3 11.6 %fusion.42 = f32[8,128]{1,0:T(8,128)S(1)} fusion(f32[6400,128,8]{1,0,2:T(8,128)} %get-tuple-element.254, f32[8,128]{1,0:T(8,128)S(1)} %get-tuple-element.255, pred[128,6400]{0,1:T(8,128)(4,1)S(1)} %fusion.40), kind=kLoop, calls=%fused_computation.9.clone.1 | loop fusion | flops 26213376 | bytes 27041792 | tf_op jit(solution)/shard_map/while/body/eval_jaxpr/reduce_sum | solution.py:37
  356.1 1.6 copy.49
  357.7 0.1 copy.48
  357.8 12.3 %fusion.43 = bf16[128,8,128]{2,0,1:T(8,128)(2,1)S(1)} fusion(f32[8,128]{1,0:T(8,128)S(1)} %fusion.42, f32[8,128]{1,0:T(8,128)S(1)} %get-tuple-element.255, f32[6400,128,8]{1,0,2:T(8,128)} %get-tuple-element.254, pred[128,6400]{0,1:T(8,128)(4,1)S(1)} %fusion.40, bf16[128,128]{0,1:T(8,128)(2,1)S(1)} %bitcast.125, ...), kind=kOutput, calls=%fused_computation.28.clone.1 | convolution fusion | flops 1715535872 | bytes 28942336 | tf_op jit(solution)/shard_map/while/body/eval_jaxpr/kgtl,lkd->tkgd/dot_general | solution.py:38
  370.2 0.1 copy.50
  370.4 0.8 copy-done.8
  371.2 0.6 dynamic_slice.72
  371.8 0.6 iota_compare_fusion.7
  372.5 5.8 fusion.40
  378.2 1.5 dynamic-slice_bitcast_fusion.8
  379.8 13.2 %fusion.41 = (f32[8,128]{1,0:T(8,128)S(1)}, f32[6400,128,8]{1,0,2:T(8,128)}) fusion(pred[128,6400]{0,1:T(8,128)(4,1)S(1)} %fusion.40, bf16[1,128,1,8,128]{4,3,1,0,2:T(8,128)(2,1)S(1)} %constant_dynamic-slice_fusion.6, bf16[128,128]{1,0:T(8,128)(2,1)S(1)} %get-tuple-element.252, bf16[128,128]{1,0:T(8,128)(2,1)S(1)} %get-tuple-element.253, ...), kind=kOutput, calls=%fused_computation.10.clone.1 | convolution fusion | flops 1702296576 | bytes 28938240 | tf_op jit(solution)/shard_map/while/body/eval_jaxpr/tkgd,lkd->kgtl/dot_general | solution.py:22
  393.0 11.6 %fusion.42 = f32[8,128]{1,0:T(8,128)S(1)} fusion(f32[6400,128,8]{1,0,2:T(8,128)} %get-tuple-element.254, f32[8,128]{1,0:T(8,128)S(1)} %get-tuple-element.255, pred[128,6400]{0,1:T(8,128)(4,1)S(1)} %fusion.40), kind=kLoop, calls=%fused_computation.9.clone.1 | loop fusion | flops 26213376 | bytes 27041792 | tf_op jit(solution)/shard_map/while/body/eval_jaxpr/reduce_sum | solution.py:37
  404.8 1.6 copy.49
  406.4 0.1 copy.48
  406.6 12.3 %fusion.43 = bf16[128,8,128]{2,0,1:T(8,128)(2,1)S(1)} fusion(f32[8,128]{1,0:T(8,128)S(1)} %fusion.42, f32[8,128]{1,0:T(8,128)S(1)} %get-tuple-element.255, f32[6400,128,8]{1,0,2:T(8,128)} %get-tuple-element.254, pred[128,6400]{0,1:T(8,128)(4,1)S(1)} %fusion.40, bf16[128,128]{0,1:T(8,128)(2,1)S(1)} %bitcast.125, ...), kind=kOutput, calls=%fused_computation.28.clone.1 | convolution fusion | flops 1715535872 | bytes 28942336 | tf_op jit(solution)/shard_map/while/body/eval_jaxpr/kgtl,lkd->tkgd/dot_general | solution.py:38
  418.9 0.1 copy.50
  419.1 0.8 copy-done.8
  419.9 0.3 all-reduce.2.cloned.1.call-start
  420.2 50.8 %all-gather.2.cloned.1.call-done = bf16[1024,1024]{1,0:T(8,128)(2,1)} async-done(((bf16[256,1024]{1,0:T(8,128)(2,1)}), bf16[1024,1024]{1,0:T(8,128)(2,1)}) %all-gather.2.cloned.1.call-update) | async-done | bytes 2097168 | tf_op jit(solution)/shard_map/all_gather | solution.py:89
  471.0 9.3 %convolution_convert_fusion = bf16[1024,2048]{1,0:T(8,128)(2,1)} fusion(bf16[1024,1024]{1,0:T(8,128)(2,1)} %all-gather.2.cloned.1.call-done, bf16[1024,2048]{1,0:T(8,128)(2,1)} %param.17), kind=kOutput, calls=%fused_computation.49 | convolution fusion | flops 4297064448 | bytes 10485760 | tf_op jit(solution)/shard_map/dot_general | solution.py:88
  480.4 84.4 %all-reduce.2.cloned.1.call-done = bf16[4,256,2048]{2,1,0:T(8,128)(2,1)} async-done(((bf16[4,256,2048]{2,1,0:T(8,128)(2,1)}), bf16[4,256,2048]{2,1,0:T(8,128)(2,1)}) %all-reduce.2.cloned.1.call-update) | async-done | bytes 4194320 | tf_op jit(solution)/shard_map/psum | solution.py:91
  564.7 97.6 %all_to_all.39 = bf16[4,256,2048]{2,1,0:T(8,128)(2,1)S(1)} all-to-all(bf16[4,256,2048]{2,1,0:T(8,128)(2,1)} %all-reduce.2.cloned.1.call-done), channel_id=1, replica_groups=mesh['fsdp'=4,'seq'=2,'head'=4] {'fsdp'}, dimensions={0} | all-to-all | bytes 8388608 | tf_op jit(solution)/shard_map/all_to_all | solution.py:92
  662.3 2.3 copy.37
  (57 shorter events, 1.1 us)
Async XLA Ops:
  6.5 18.5 %copy-start = (bf16[64,128,128]{2,1,0:T(8,128)(2,1)S(1)}, bf16[64,128,128]{2,1,0:T(8,128)(2,1)}, u32[]{:S(2)}) copy-start(bf16[64,128,128]{2,1,0:T(8,128)(2,1)} %param.14) | copy-start | bytes 6291460
  33.1 4.9 copy-start.3
  33.1 141.9 %all-to-all-start.1 = ((bf16[192,128,128]{2,1,0:T(8,128)(2,1)}), bf16[192,128,128]{2,1,0:T(8,128)(2,1)}, u32[]{:S(2)}, u32[]{:S(2)}) async-start(bf16[192,128,128]{2,1,0:T(8,128)(2,1)} %gather_fusion.1), calls=%async_computation.1 | async-start | bytes 12582912 | tf_op jit(solution)/shard_map/all_to_all | solution.py:66
  45.9 133.8 %copy-start.4 = (bf16[256,128]{1,0:T(8,128)(2,1)S(1)}, bf16[256,128]{1,0:T(8,128)(2,1)}, u32[]{:S(2)}) copy-start(bf16[256,128]{1,0:T(8,128)(2,1)} %param.12) | copy-start | bytes 196612
  45.9 137.7 %copy-start.5 = (bf16[256,128]{1,0:T(8,128)(2,1)S(1)}, bf16[256,128]{1,0:T(8,128)(2,1)}, u32[]{:S(2)}) copy-start(bf16[256,128]{1,0:T(8,128)(2,1)} %param.11) | copy-start | bytes 196612
  45.9 141.5 %copy-start.6 = (bf16[256,1024]{1,0:T(8,128)(2,1)S(1)}, bf16[256,1024]{1,0:T(8,128)(2,1)}, u32[]{:S(2)}) copy-start(bf16[256,1024]{1,0:T(8,128)(2,1)} %param.10) | copy-start | bytes 1572868
  175.0 142.0 %all-to-all-start.2 = ((bf16[192,128,128]{2,1,0:T(8,128)(2,1)}), bf16[192,128,128]{2,1,0:T(8,128)(2,1)}, u32[]{:S(2)}, u32[]{:S(2)}) async-start(bf16[192,128,128]{2,1,0:T(8,128)(2,1)} %gather_fusion.3), calls=%async_computation.2 | async-start | bytes 12582912 | tf_op jit(solution)/shard_map/all_to_all | solution.py:65
  179.7 291.3 %all-gather.2.cloned.1.call-start = ((), (), s32[]{:S(2)}) async-start(), calls=%async_computation.4 | async-start | bytes 2621440 | tf_op jit(solution)/shard_map/all_gather | solution.py:89
  179.9 51.3 %collective-permute-start = (bf16[128,128]{0,1:T(8,128)(2,1)S(1)}, bf16[128,128]{0,1:T(8,128)(2,1)S(1)}, u32[]{:S(2)}, u32[]{:S(2)}) collective-permute-start(bf16[128,128]{0,1:T(8,128)(2,1)S(1)} %copy.35), channel_id=1, source_target_pairs={{0,4},{4,8},{8,12},{12,16},{16,20},{20,24},{24,28},{1,5},{5,9},{9,... | collective-permute-start | bytes 98312 | tf_op jit(solution)/shard_map/ppermute | solution.py:12
  183.7 48.0 %collective-permute-start.1 = (bf16[128,128]{1,0:T(8,128)(2,1)S(1)}, bf16[128,128]{1,0:T(8,128)(2,1)S(1)}, u32[]{:S(2)}, u32[]{:S(2)}) collective-permute-start(bf16[128,128]{1,0:T(8,128)(2,1)S(1)} %get-tuple-element.177), channel_id=1, source_target_pairs={{0,4},{4,8},{8,12},{12,16},{16,20},{20,24},{24,28},{1,5},{5,9},{9,... | collective-permute-start | bytes 98312 | tf_op jit(solution)/shard_map/ppermute | solution.py:12
  344.3 11.6 %copy-start.2 = (bf16[2,6144,128]{2,1,0:T(8,128)(2,1)S(1)}, bf16[2,6144,128]{2,1,0:T(8,128)(2,1)}, u32[]{:S(2)}) copy-start(bf16[2,6144,128]{2,1,0:T(8,128)(2,1)} %get-tuple-element.280) | copy-start | bytes 9437188 | tf_op jit(solution)/shard_map/while
  357.8 12.5 %copy-start.7 = (bf16[2,128,1024]{2,1,0:T(8,128)(2,1)S(1)}, bf16[2,128,1024]{2,1,0:T(8,128)(2,1)}, u32[]{:S(2)}) copy-start(bf16[2,128,1024]{2,1,0:T(8,128)(2,1)} %get-tuple-element.268) | copy-start | bytes 1572868 | tf_op jit(solution)/shard_map/while
  370.4 0.8 copy-start.8
  393.0 11.6 %copy-start.2 = (bf16[2,6144,128]{2,1,0:T(8,128)(2,1)S(1)}, bf16[2,6144,128]{2,1,0:T(8,128)(2,1)}, u32[]{:S(2)}) copy-start(bf16[2,6144,128]{2,1,0:T(8,128)(2,1)} %get-tuple-element.280) | copy-start | bytes 9437188 | tf_op jit(solution)/shard_map/while
  406.6 12.5 %copy-start.7 = (bf16[2,128,1024]{2,1,0:T(8,128)(2,1)S(1)}, bf16[2,128,1024]{2,1,0:T(8,128)(2,1)}, u32[]{:S(2)}) copy-start(bf16[2,128,1024]{2,1,0:T(8,128)(2,1)} %get-tuple-element.268) | copy-start | bytes 1572868 | tf_op jit(solution)/shard_map/while
  419.1 0.8 copy-start.8
  419.9 144.8 %all-reduce.2.cloned.1.call-start = ((), (), s32[]{:S(2)}) async-start(), calls=%async_computation.5 | async-start | bytes 8388608 | tf_op jit(solution)/shard_map/psum | solution.py:91
  662.3 2.3 copy-start.1
Sparse Core Ops, SparseCore 0:
  420.1 50.9 all-gather.1
  480.5 84.1 all-reduce.1
where the time goes:
time: 672 us
  waiting for transfers between devices  388 us (58%)
  blocking collectives  111 us (17%)
  matrix products  60.5 us (9%)
  local copies, waits for them, and re-layouts  43.7 us (7%)
  other arithmetic  37 us (6%)
  starting transfers between devices  17.3 us (3%)
  between operations  13.6 us (2%)
    all_to_all x1, waiting for transfers between devices, body(): lax.all_to_all(send_v, ('fsdp', 'seq'), split_axis=0, concat_axis=0, tile...  129 us
    all_to_all x1, blocking collectives, body(): lax.all_to_all(summed, 'fsdp', split_axis=0, concat_axis=1, tiled=True)  97.6 us
    psum x1, waiting for transfers between devices, body(): summed = lax.psum(partial_terms.astype(jnp.bfloat16), 'head')  84.4 us
    all_to_all x1, waiting for transfers between devices, body(): lax.all_to_all(send_k, ('fsdp', 'seq'), split_axis=0, concat_axis=0, tile...  79.8 us
    all_gather x1, waiting for transfers between devices, body(): lax.all_gather(attended, 'fsdp', axis=0, tiled=True)  50.8 us
    ppermute x2, waiting for transfers between devices, from_behind(): lax.ppermute(value, axis, [(source, source + steps) for source in range(l...  44.2 us
    dot_general x2, matrix products, attend_block(): jnp.einsum('tkgd,lkd->kgtl', query_block, keys_four, preferred_element_ty...  26.5 us
    dot_general x2, matrix products, attend_block(): jnp.einsum('kgtl,lkd->tkgd', probs_bf, values_four, preferred_element_typ...  24.7 us
  transfers between devices with their start and end apart: 6, of which 6 were waited for; matrix products, arithmetic and copies ran while one was open for 2% of the time, Pallas kernels for 0%

commit v1 on v0

v1 whole, which is shorter than its diff:
```python
import functools
import math

import jax
import jax.numpy as jnp
from jax import lax
from jax.experimental import pallas as pl
from jax.experimental.pallas import tpu as pltpu
from jax.sharding import PartitionSpec as P

HD = 128
NEG = -1e30
F32 = jnp.float32
BF16 = jnp.bfloat16
VMEM_LIMIT = 48 * 1024 * 1024


def swap(value, axis, distance):
    count = lax.axis_size(axis)
    return lax.ppermute(value, axis, [(i, i ^ distance) for i in range(count)])


def stack_heads(q_ref, stacked):
    tokens = q_ref.shape[0]
    for h in range(q_ref.shape[1] // HD):
        stacked[h * tokens:(h + 1) * tokens, :] = q_ref[:, h * HD:(h + 1) * HD]


def write_partial(out_ref, acc, top):
    tokens = out_ref.shape[0]
    heads = (out_ref.shape[1] - HD) // HD
    lane = lax.broadcasted_iota(jnp.int32, (tokens, HD), 1)
    stats = jnp.zeros((tokens, HD), F32)
    for h in range(heads):
        rows = slice(h * tokens, (h + 1) * tokens)
        total = acc[rows, HD:]
        inverse = jnp.where(total > 0, 1.0 / total, 0.0)
        out_ref[:, h * HD:(h + 1) * HD] = (acc[rows, :HD] * inverse).astype(BF16)
        high = total.astype(BF16).astype(F32)
        stats = jnp.where(lane == h, top[rows, :].astype(F32), stats)
        stats = jnp.where(lane == heads + h, high, stats)
        stats = jnp.where(lane == 2 * heads + h, total - high, stats)
    out_ref[:, heads * HD:] = stats.astype(BF16)


def add_pair(acc, probs, values):
    ones = jnp.ones(values.shape, BF16)
    acc[...] += jnp.dot(probs, jnp.concatenate([values, ones], axis=1), preferred_element_type=F32)


def scaled_scores(stacked, keys):
    scores = lax.dot_general(stacked, keys, (((1,), (1,)), ((), ())), preferred_element_type=F32)
    return scores * (math.log2(math.e) / math.sqrt(HD))


def listed_kernel(blocks, table, *refs):
    q_refs, refs = refs[:blocks], refs[blocks:]
    k_hbm, v_hbm, refs = refs[0], refs[1], refs[2:]
    out_refs, refs = refs[:blocks], refs[blocks:]
    k_buf, v_buf, stacked, scores, acc, running, top, sems = refs
    block_len = k_hbm.shape[1]

    def pairs(j):
        return (table[j, 0] + 1) // 2

    def copies(j, i):
        slot, side = table[j, 1 + i], j % 2
        return (
            pltpu.make_async_copy(k_hbm.at[slot], k_buf.at[side, i], sems.at[side, 0]),
            pltpu.make_async_copy(v_hbm.at[slot], v_buf.at[side, i], sems.at[side, 1]),
        )

    def fetch(j):
        def one(i, carry):
            for copy in copies(j, i):
                copy.start()
            return carry
        lax.fori_loop(0, 2 * pairs(j), one, 0)

    def arrived(j):
        def one(i, carry):
            for copy in copies(j, i):
                copy.wait()
            return carry
        lax.fori_loop(0, 2 * pairs(j), one, 0)

    fetch(0)
    for j in range(blocks):
        side = j % 2
        if j + 1 < blocks:
            fetch(j + 1)
        stack_heads(q_refs[j], stacked)
        running[...] = jnp.full(running.shape, NEG, F32)
        acc[...] = jnp.zeros(acc.shape, F32)
        arrived(j)

        def first(i, carry):
            keys = k_buf[side, pl.ds(2 * i, 2)].reshape(2 * block_len, HD)
            found = scaled_scores(stacked[...], keys)
            bias = jnp.where(2 * i + 1 < table[j, 0], 0.0, NEG).astype(F32)
            one, two = found[:, :block_len], found[:, block_len:] + bias
            scores[i, :, :block_len] = one
            scores[i, :, block_len:] = two
            running[...] = jnp.maximum(running[...], jnp.maximum(one, two))
            return carry

        lax.fori_loop(0, pairs(j), first, 0)
        top[...] = jnp.broadcast_to(jnp.max(running[...], axis=1, keepdims=True), top.shape).astype(BF16)

        def second(i, carry):
            reference = top[...].astype(F32)
            probs = jnp.concatenate(
                [jnp.exp2(scores[i, :, :block_len] - reference), jnp.exp2(scores[i, :, block_len:] - reference)], axis=1
            ).astype(BF16)
            add_pair(acc, probs, v_buf[side, pl.ds(2 * i, 2)].reshape(2 * block_len, HD))
            return carry

        lax.fori_loop(0, pairs(j), second, 0)
        write_partial(out_refs[j], acc, top)


def attend_listed(table, queries, cache_k, cache_v):
    blocks = len(queries)
    tokens, columns = queries[0].shape
    rows = tokens * columns // HD
    block_len = cache_k.shape[1]
    capacity = table.shape[1] - 1
    vmem = pl.BlockSpec(memory_space=pltpu.VMEM)
    hbm = pl.BlockSpec(memory_space=pl.ANY)
    keys = blocks * block_len * 6
    return pl.pallas_call(
        functools.partial(listed_kernel, blocks),
        out_shape=[jax.ShapeDtypeStruct((tokens, columns + HD), BF16)] * blocks,
        in_specs=[pl.BlockSpec(memory_space=pltpu.SMEM)] + [vmem] * blocks + [hbm] * 2,
        out_specs=[vmem] * blocks,
        scratch_shapes=[
            pltpu.VMEM((2, capacity, block_len, HD), BF16),
            pltpu.VMEM((2, capacity, block_len, HD), BF16),
            pltpu.VMEM((rows, HD), BF16),
            pltpu.VMEM((capacity // 2, rows, 2 * block_len), F32),
            pltpu.VMEM((rows, 2 * HD), F32),
            pltpu.VMEM((rows, HD), F32),
            pltpu.VMEM((rows, HD), BF16),
            pltpu.SemaphoreType.DMA((2, 2)),
        ],
        compiler_params=pltpu.CompilerParams(vmem_limit_bytes=VMEM_LIMIT),
        cost_estimate=pl.CostEstimate(
            flops=4 * rows * keys * HD * 2, bytes_accessed=4 * keys * HD + 4 * blocks * rows * HD, transcendentals=rows * keys
        ),
    )(table, *queries, cache_k, cache_v)


def span_kernel(flag, q_ref, k0, k1, v0, v1, out_ref, stacked, acc, top):
    tokens = q_ref.shape[0]
    stack_heads(q_ref, stacked)
    keys = jnp.concatenate([k0[...], k1[...]], axis=0)
    found = scaled_scores(stacked[...], keys)
    row = lax.broadcasted_iota(jnp.int32, found.shape, 0) % tokens
    column = lax.broadcasted_iota(jnp.int32, found.shape, 1)
    behind = jnp.where(flag[0] > 0, tokens, 0)
    allowed = (column < behind) | ((column >= tokens) & (column - tokens <= row))
    found = jnp.where(allowed, found, NEG)
    top[...] = jnp.broadcast_to(jnp.max(found, axis=1, keepdims=True), top.shape).astype(BF16)
    reference = jnp.concatenate([top[...], top[...]], axis=1).astype(F32)
    acc[...] = jnp.zeros(acc.shape, F32)
    add_pair(acc, jnp.exp2(found - reference).astype(BF16), jnp.concatenate([v0[...], v1[...]], axis=0))
    write_partial(out_ref, acc, top)


def attend_span(flag, queries, k0, k1, v0, v1):
    tokens, columns = queries.shape
    rows = tokens * columns // HD
    vmem = pl.BlockSpec(memory_space=pltpu.VMEM)
    return pl.pallas_call(
        span_kernel,
        out_shape=jax.ShapeDtypeStruct((tokens, columns + HD), BF16),
        in_specs=[pl.BlockSpec(memory_space=pltpu.SMEM)] + [vmem] * 5,
        out_specs=vmem,
        scratch_shapes=[pltpu.VMEM((rows, HD), BF16), pltpu.VMEM((rows, 2 * HD), F32), pltpu.VMEM((rows, HD), BF16)],
        compiler_params=pltpu.CompilerParams(vmem_limit_bytes=VMEM_LIMIT),
        cost_estimate=pl.CostEstimate(flops=8 * rows * tokens * HD, bytes_accessed=6 * rows * HD, transcendentals=2 * rows * tokens),
    )(flag, queries, k0, k1, v0, v1)


def merge_kernel(count, final, *refs):
    parts, out_ref = refs[:count], refs[count]
    tokens = out_ref.shape[0]
    heads = (parts[0].shape[1] - HD) // HD
    stats = [part[:, heads * HD:].astype(F32) for part in parts]
    sums = [pltpu.roll(s, HD - heads, 1) + pltpu.roll(s, HD - 2 * heads, 1) for s in stats]
    top = functools.reduce(jnp.maximum, stats)
    weights = [jnp.exp2(s - top) * l for s, l in zip(stats, sums)]
    total = functools.reduce(jnp.add, weights)
    inverse = jnp.where(total > 0, 1.0 / total, 0.0)
    weights = [w * inverse for w in weights]
    for h in range(heads):
        columns = slice(h * HD, (h + 1) * HD)
        out_ref[:, columns] = functools.reduce(
            jnp.add, [w[:, h:h + 1] * part[:, columns].astype(F32) for w, part in zip(weights, parts)]
        ).astype(BF16)
    if not final:
        lane = lax.broadcasted_iota(jnp.int32, (tokens, HD), 1)
        high = total.astype(BF16).astype(F32)
        merged = jnp.where(lane < heads, top, pltpu.roll(high, heads, 1))
        merged = jnp.where(lane < 2 * heads, merged, pltpu.roll(total - high, 2 * heads, 1))
        out_ref[:, heads * HD:] = jnp.where(lane < 3 * heads, merged, 0.0).astype(BF16)


def merge(parts, final):
    tokens, columns = parts[0].shape
    vmem = pl.BlockSpec(memory_space=pltpu.VMEM)
    return pl.pallas_call(
        functools.partial(merge_kernel, len(parts), final),
        out_shape=jax.ShapeDtypeStruct((tokens, columns - HD if final else columns), BF16),
        in_specs=[vmem] * len(parts),
        out_specs=vmem,
        compiler_params=pltpu.CompilerParams(vmem_limit_bytes=VMEM_LIMIT),
        cost_estimate=pl.CostEstimate(
            flops=2 * len(parts) * tokens * columns, bytes_accessed=2 * (len(parts) + 1) * tokens * columns, transcendentals=0
        ),
    )(*parts)


def place_kernel(pieces, chunk, offsets, *refs):
    out_ref, buffer, sem = refs[-3:]
    n_z = refs[0].shape[0]
    tokens, width = refs[0].shape[1:]
    for j in range(pieces):
        for k in range(n_z):
            start = pl.multiple_of(offsets[j, k], width)
            buffer[:, pl.ds(start, width)] = refs[j][k]
    copy = pltpu.make_async_copy(buffer, out_ref.at[pl.ds(chunk * tokens, tokens)], sem)
    copy.start()
    copy.wait()


def place(offsets, pieces, chunk, chunks, before):
    n_z, tokens, width = pieces[0].shape
    columns = n_z * len(pieces) * width
    vmem = pl.BlockSpec(memory_space=pltpu.VMEM)
    hbm = pl.BlockSpec(memory_space=pl.ANY)
    held = [] if before is None else [before]
    return pl.pallas_call(
        functools.partial(place_kernel, len(pieces), chunk),
        out_shape=jax.ShapeDtypeStruct((chunks * tokens, columns), BF16),
        in_specs=[pl.BlockSpec(memory_space=pltpu.SMEM)] + [vmem] * len(pieces) + [hbm] * len(held),
        out_specs=hbm,
        scratch_shapes=[pltpu.VMEM((tokens, columns), BF16), pltpu.SemaphoreType.DMA],
        input_output_aliases={1 + len(pieces): 0} if held else {},
        compiler_params=pltpu.CompilerParams(vmem_limit_bytes=VMEM_LIMIT),
        cost_estimate=pl.CostEstimate(flops=0, bytes_accessed=4 * tokens * columns, transcendentals=0),
    )(offsets, *pieces, *held)


def body(queries, span_k, span_v, cache_k, cache_v, block_slot, pattern, wo):
    n_z, n_x, n_h = (lax.axis_size(a) for a in ("fsdp", "seq", "head"))
    z, x, me = (lax.axis_index(a) for a in ("fsdp", "seq", "head"))
    chunks, list_len = pattern.shape
    cb_local, block_len, _ = cache_k.shape
    index_here = z * n_x + x
    capacity = max(2, 2 * chunks * list_len // (n_z * n_x))
    capacity = min(capacity, list_len)
    capacity += capacity % 2

    slots = lax.all_gather(block_slot[pattern], ("fsdp", "seq"), axis=0, tiled=True)
    order = jnp.stack([
        ((z ^ k) * n_x + (x ^ s)) * chunks + c for c in range(chunks) for s in range(n_x) for k in range(n_z)
    ])
    slots = slots[order]
    within = slots - index_here * cb_local
    mine = (within >= 0) & (within < cb_local)
    rank = jnp.sum((mine[:, None, :] & jnp.tri(list_len, list_len, -1, dtype=bool)[None]).astype(jnp.int32), axis=2)
    place_of = jnp.where(mine, rank, -1)
    compact = jnp.sum(jnp.where(place_of[:, None, :] == jnp.arange(capacity)[None, :, None], within[:, None, :], 0), axis=2)
    table = jnp.concatenate([jnp.sum(mine.astype(jnp.int32), axis=1, keepdims=True), compact], axis=1)
    table = table.reshape(chunks, n_x, n_z, capacity + 1)

    n_index = n_z * n_x
    prior = lax.ppermute(
        jnp.concatenate([span_k[-block_len:], span_v[-block_len:]], axis=1),
        ("fsdp", "seq"), [(i, i + 1) for i in range(n_index - 1)],
    )

    quarter = wo.shape[1] // n_h
    columns_of = [lax.dynamic_slice_in_dim(wo, (me ^ j) * quarter, quarter, axis=1) for j in range(n_h)]
    offsets = jnp.stack([jnp.stack([(z ^ k) * wo.shape[1] + (me ^ j) * quarter for k in range(n_z)]) for j in range(n_h)])

    mixed = None
    for c in range(chunks):
        rows = slice(c * block_len, (c + 1) * block_len)
        own = queries[rows]
        by_z = [own] + [swap(own, "fsdp", k) for k in range(1, n_z)]
        if c == 0:
            k0, v0 = prior[:, :HD], prior[:, HD:]
        else:
            before = slice((c - 1) * block_len, c * block_len)
            k0, v0 = span_k[before], span_v[before]
        flag = (index_here * chunks + c > 0).astype(jnp.int32).reshape(1)
        span_part = attend_span(flag, own, k0, span_k[rows], v0, span_v[rows])
        gathered = [[swap(q, "seq", s) for q in by_z] for s in range(1, n_x)]
        away = [attend_listed(table[c, s], gathered[s - 1], cache_k, cache_v) for s in range(1, n_x)]
        here = attend_listed(table[c, 0], by_z, cache_k, cache_v)
        parts = [[here[k]] + [swap(away[s - 1][k], "seq", s) for s in range(1, n_x)] for k in range(n_z)]
        returned = [swap(merge(parts[k], False), "fsdp", k) for k in range(1, n_z)]
        attended = merge(returned + parts[0] + [span_part], True)

        all_z = jnp.concatenate([attended] + [swap(attended, "fsdp", k) for k in range(1, n_z)], axis=0)
        terms = [jnp.dot(all_z, w, preferred_element_type=F32).astype(BF16) for w in columns_of]
        distance = 1
        while distance < n_h:
            kept = [j for j in range(0, n_h, 2 * distance)]
            got = swap(jnp.concatenate([terms[j + distance] for j in kept], axis=1), "head", distance)
            for at, j in enumerate(kept):
                terms[j] = (terms[j].astype(F32) + got[:, at * quarter:(at + 1) * quarter].astype(F32)).astype(BF16)
            distance *= 2
        summed = terms[0].reshape(n_z, block_len, quarter)
        pieces = [jnp.stack([summed[0]] + [swap(summed[k], "fsdp", k) for k in range(1, n_z)])]
        while distance > 1:
            distance //= 2
            got = swap(jnp.stack(pieces), "head", distance)
            pieces = pieces + [got[i] for i in range(len(pieces))]
        step, names = n_h, [0]
        while step > 1:
            step //= 2
            names = names + [i ^ step for i in names]
        pieces = [pieces[names.index(j)] for j in range(n_h)]
        mixed = place(offsets, pieces, c, chunks, mixed)
    return mixed


def solution(mesh):
    return jax.shard_map(
        body,
        mesh=mesh,
        in_specs=(
            P(("fsdp", "seq"), "head"),
            P(("fsdp", "seq"), "head"),
            P(("fsdp", "seq"), "head"),
            P(("fsdp", "seq"), None, "head"),
            P(("fsdp", "seq"), None, "head"),
            P(),
            P(("fsdp", "seq"), None),
            P("head", "fsdp"),
        ),
        out_specs=P(("fsdp", "seq"), None),
        check_vma=False,
    )
```

time: 672 us -> 292 us (0.43)
  waiting for transfers between devices: 388 us -> 75 us
  blocking collectives: 111 us -> 30.2 us
  starting transfers between devices: 17.3 us -> 95.5 us
  Pallas kernels: 0 us -> 63.3 us
  matrix products: 60.5 us -> 12.4 us
  local copies, waits for them, and re-layouts: 43.7 us -> 7.94 us
  other arithmetic: 37 us -> 4.44 us
  between operations: 13.6 us -> 0.95 us
    all_to_all x2 -> x0, waiting for transfers between devices: 209 us -> none  [the longest x1 129 us: body(): lax.all_to_all(send_v, ('fsdp', 'seq'), split_axis=0, concat_axis=0, tile...]
    all_to_all x2 -> x0, blocking collectives: 111 us -> none  [the longest x1 97.6 us: body(): lax.all_to_all(summed, 'fsdp', split_axis=0, concat_axis=1, tiled=True)]
    ppermute x2 -> x49, starting transfers between devices: 7.31 us -> 95.5 us  [the longest x48 91.8 us: swap(): return lax.ppermute(value, axis, [(i, i ^ distance) for i in range(count)])]
    psum x1 -> x0, waiting for transfers between devices: 84.4 us -> none  [body(): summed = lax.psum(partial_terms.astype(jnp.bfloat16), 'head')]
    pallas_call x0 -> x16, Pallas kernels: none -> 63.3 us  [the longest x4 50.4 us: attend_listed(): pl.pallas_call(functools.partial(listed_kernel, blocks), out_shape=[jax.S...]
    all_gather x1 -> x0, waiting for transfers between devices: 50.8 us -> none  [body(): lax.all_gather(attended, 'fsdp', axis=0, tiled=True)]
    dot_general x5 -> x8, matrix products: 60.5 us -> 12.4 us  [body(): jnp.dot(all_z, w, preferred_element_type=F32).astype(BF16)]
    ppermute x2 -> x49, waiting for transfers between devices: 44.2 us -> 75 us  [the longest x48 75 us: swap(): return lax.ppermute(value, axis, [(i, i ^ distance) for i in range(count)])]
  transfers between devices with their start and end apart: 6 -> 49, of which waited for: 6 -> 14; matrix products, arithmetic and copies ran while one was open for 2% -> 7% of each run, Pallas kernels for 0% -> 21%
where the time goes in v1:
time: 292 us; the launch traced here: 290 us
  starting transfers between devices  95.5 us (33%)
  waiting for transfers between devices  75 us (26%)
  Pallas kernels  63.3 us (22%)
  blocking collectives  30.2 us (10%)
  matrix products  12.4 us (4%)
  local copies, waits for them, and re-layouts  7.94 us (3%)
  other arithmetic  4.44 us (2%)
    ppermute x48, starting transfers between devices, swap(): return lax.ppermute(value, axis, [(i, i ^ distance) for i in range(count)])  91.8 us
    ppermute x48, waiting for transfers between devices, swap(): return lax.ppermute(value, axis, [(i, i ^ distance) for i in range(count)])  75 us
    pallas_call x4, Pallas kernels, attend_listed(): pl.pallas_call(functools.partial(listed_kernel, blocks), out_shape=[jax.S...  50.4 us
    all_gather x1, blocking collectives, body(): lax.all_gather(block_slot[pattern], ('fsdp', 'seq'), axis=0, tiled=True)  30.2 us
    dot_general x8, matrix products, body(): jnp.dot(all_z, w, preferred_element_type=F32).astype(BF16)  12.4 us
    pallas_call x8, Pallas kernels, merge(): pl.pallas_call(functools.partial(merge_kernel, len(parts), final), out_sh...  7.28 us
  transfers between devices with their start and end apart: 49, of which 14 were waited for; matrix products, arithmetic and copies ran while one was open for 7% of the time, Pallas kernels for 21%

profile of v1, /device:TPU:0, one launch (start us, length us, event | category | flops | bytes accessed | tf_op | source)
XLA Modules:
  0.0 289.7 jit_solution(4161845177036633082)
XLA Ops:
  1.2 3.0 %collective-permute-start.27 = (bf16[128,1024]{1,0:T(8,128)(2,1)S(1)}, bf16[128,1024]{1,0:T(8,128)(2,1)}, u32[]{:S(2)}, u32[]{:S(2)}) collective-permute-start(bf16[128,1024]{1,0:T(8,128)(2,1)S(1)} %get-tuple-element.50.refs_0_.q_ref), channel_id=1, source_target_pairs={{0,4},{4,0},{1,5},{5,1},{2,6},{6,2},{3,7},{7,3},{8,12},{12,8},{9,1... | collective-permute-start | bytes 786440 | tf_op jit(solution)/shard_map/ppermute | solution.py:20
  4.2 3.6 %collective-permute-start.26 = (bf16[128,1024]{1,0:T(8,128)(2,1)S(1)}, bf16[128,1024]{1,0:T(8,128)(2,1)S(1)}, u32[]{:S(2)}, u32[]{:S(2)}) collective-permute-start(bf16[128,1024]{1,0:T(8,128)(2,1)S(1)} %get-tuple-element.50.refs_0_.q_ref), channel_id=1, source_target_pairs={{0,24},{8,16},{16,8},{24,0},{1,25},{9,17},{17,9},{25,1},{2,26},{10... | collective-permute-start | bytes 786440 | tf_op jit(solution)/shard_map/ppermute | solution.py:20
  8.6 3.6 %collective-permute-start.2 = (bf16[128,1024]{1,0:T(8,128)(2,1)S(1)}, bf16[128,1024]{1,0:T(8,128)(2,1)S(1)}, u32[]{:S(2)}, u32[]{:S(2)}) collective-permute-start(bf16[128,1024]{1,0:T(8,128)(2,1)S(1)} %get-tuple-element.51.refs_0_.q_ref), channel_id=1, source_target_pairs={{0,24},{8,16},{16,8},{24,0},{1,25},{9,17},{17,9},{25,1},{2,26},{10... | collective-permute-start | bytes 786440 | tf_op jit(solution)/shard_map/ppermute | solution.py:20
  14.6 30.2 %all-gather.1 = s32[8,2,48]{2,1,0:T(2,128)S(1)} all-gather(s32[1,2,48]{2,1,0:T(2,128)S(1)} %reshape.700), channel_id=2, replica_groups=mesh['fsdp'=4,'seq'=2,'head'=4] {'fsdp','seq'}, dimensions={0}, use_global_device_ids=true | all-gather | bytes 3456 | tf_op jit(solution)/shard_map/all_gather | solution.py:265
  45.9 6.9 %collective-permute-start.1 = (bf16[128,1024]{1,0:T(8,128)(2,1)S(1)}, bf16[128,1024]{1,0:T(8,128)(2,1)}, u32[]{:S(2)}, u32[]{:S(2)}) collective-permute-start(bf16[128,1024]{1,0:T(8,128)(2,1)S(1)} %get-tuple-element.51.refs_0_.q_ref), channel_id=1, source_target_pairs={{0,16},{8,24},{16,0},{24,8},{1,17},{9,25},{17,1},{25,9},{2,18},{10... | collective-permute-start | bytes 786440 | tf_op jit(solution)/shard_map/ppermute | solution.py:20
  57.3 4.2 %collective-permute-done.1.refs_2_ = bf16[128,1024]{1,0:T(8,128)(2,1)} collective-permute-done((bf16[128,1024]{1,0:T(8,128)(2,1)S(1)}, bf16[128,1024]{1,0:T(8,128)(2,1)}, u32[]{:S(2)}, u32[]{:S(2)}) %collective-permute-start.1) | collective-permute-done | bytes 262176 | tf_op jit(solution)/shard_map/ppermute | solution.py:20
  61.7 3.7 %collective-permute-start.38 = (bf16[128,256]{1,0:T(8,128)(2,1)S(1)}, bf16[128,256]{1,0:T(8,128)(2,1)S(1)}, u32[]{:S(2)}, u32[]{:S(2)}) collective-permute-start(bf16[128,256]{1,0:T(8,128)(2,1)S(1)} %pad_maximum_fusion.8), channel_id=1, source_target_pairs={{0,4},{4,8},{8,12},{12,16},{16,20},{20,24},{24,28},{1,5},{5,9},{9,... | collective-permute-start | bytes 196616 | tf_op jit(solution)/shard_map/ppermute | solution.py:279
  66.6 1.7 collective-permute-done.29.refs_2_
  69.0 5.0 %collective-permute-done.28.refs_1_ = bf16[128,1024]{1,0:T(8,128)(2,1)} collective-permute-done((bf16[128,1024]{1,0:T(8,128)(2,1)}, bf16[128,1024]{1,0:T(8,128)(2,1)}, u32[]{:S(2)}, u32[]{:S(2)}) %collective-permute-start.28) | collective-permute-done | bytes 262176 | tf_op jit(solution)/shard_map/ppermute | solution.py:20
  74.6 13.9 %shard_map.90 = (bf16[128,1152]{1,0:T(8,128)(2,1)S(1)}, bf16[128,1152]{1,0:T(8,128)(2,1)S(1)}, bf16[128,1152]{1,0:T(8,128)(2,1)S(1)}, bf16[128,1152]{1,0:T(8,128)(2,1)S(1)}) custom-call(s32[4,25]{1,0:T(4,128)S(1)} %get-tuple-element.64.table, bf16[128,1024]{1,0:T(8,128)(2,1)} %collective-permute-done.27.refs_0_, ...), custom_call_target="tpu_custom_call" | custom-call | flops 3221225472 | bytes 3670016 | tf_op jit(solution)/shard_map/pallas_call | solution.py:131
  88.6 5.8 %collective-permute-start.35 = (bf16[128,1152]{1,0:T(8,128)(2,1)S(1)}, bf16[128,1152]{1,0:T(8,128)(2,1)S(1)}, u32[]{:S(2)}, u32[]{:S(2)}) collective-permute-start(bf16[128,1152]{1,0:T(8,128)(2,1)S(1)} %get-tuple-element.34), channel_id=1, source_target_pairs={{0,4},{4,0},{1,5},{5,1},{2,6},{6,2},{3,7},{7,3},{8,12},{12,8},{9,1... | collective-permute-start | bytes 884744 | tf_op jit(solution)/shard_map/ppermute | solution.py:20
  94.5 13.2 %shard_map.83 = (bf16[128,1152]{1,0:T(8,128)(2,1)}, bf16[128,1152]{1,0:T(8,128)(2,1)S(1)}, bf16[128,1152]{1,0:T(8,128)(2,1)S(1)}, bf16[128,1152]{1,0:T(8,128)(2,1)S(1)}) custom-call(s32[4,25]{1,0:T(4,128)S(1)} %get-tuple-element.66.table, bf16[128,1024]{1,0:T(8,128)(2,1)S(1)} %collective-permute-done.3.refs_0_, ...), custom_call_target="tpu_custom_call" | custom-call | flops 3221225472 | bytes 3670016 | tf_op jit(solution)/shard_map/pallas_call | solution.py:131
  107.7 4.4 %collective-permute-start.7 = (bf16[128,1152]{1,0:T(8,128)(2,1)S(1)}, bf16[128,1152]{1,0:T(8,128)(2,1)S(1)}, u32[]{:S(2)}, u32[]{:S(2)}) collective-permute-start(bf16[128,1152]{1,0:T(8,128)(2,1)S(1)} %get-tuple-element.22), channel_id=1, source_target_pairs={{0,4},{4,0},{1,5},{5,1},{2,6},{6,2},{3,7},{7,3},{8,12},{12,8},{9,1... | collective-permute-start | bytes 884744 | tf_op jit(solution)/shard_map/ppermute | solution.py:20
  112.2 1.9 collective-permute-start.31
  114.2 12.1 %shard_map.89 = (bf16[128,1152]{1,0:T(8,128)(2,1)S(1)}, bf16[128,1152]{1,0:T(8,128)(2,1)S(1)}, bf16[128,1152]{1,0:T(8,128)(2,1)S(1)}, bf16[128,1152]{1,0:T(8,128)(2,1)S(1)}) custom-call(s32[4,25]{1,0:T(4,128)S(1)} %get-tuple-element.67.table, bf16[128,1024]{1,0:T(8,128)(2,1)S(1)} %get-tuple-element.50.refs_0_.q_ref, ...), custom_call_target="tpu_custom_call" | custom-call | flops 3221225472 | bytes 3670016 | tf_op jit(solution)/shard_map/pallas_call | solution.py:131
  126.8 5.8 %collective-permute-done.31.refs_1_ = bf16[128,1152]{1,0:T(8,128)(2,1)S(1)} collective-permute-done((bf16[128,1152]{1,0:T(8,128)(2,1)S(1)}, bf16[128,1152]{1,0:T(8,128)(2,1)S(1)}, u32[]{:S(2)}, u32[]{:S(2)}) %collective-permute-start.31) | collective-permute-done | bytes 294944 | tf_op jit(solution)/shard_map/ppermute | solution.py:20
  132.7 1.8 collective-permute-start.11
  135.9 1.7 collective-permute-start.37
  138.3 4.3 %collective-permute-start.36 = (bf16[128,1152]{1,0:T(8,128)(2,1)S(1)}, bf16[128,1152]{1,0:T(8,128)(2,1)}, u32[]{:S(2)}, u32[]{:S(2)}) collective-permute-start(bf16[128,1152]{1,0:T(8,128)(2,1)S(1)} %shard_map.93), channel_id=1, source_target_pairs={{0,24},{8,16},{16,8},{24,0},{1,25},{9,17},{17,9},{25,1},{2,26},{10... | collective-permute-start | bytes 884744 | tf_op jit(solution)/shard_map/ppermute | solution.py:20
  142.6 11.2 %shard_map.82 = (bf16[128,1152]{1,0:T(8,128)(2,1)S(1)}, bf16[128,1152]{1,0:T(8,128)(2,1)S(1)}, bf16[128,1152]{1,0:T(8,128)(2,1)S(1)}, bf16[128,1152]{1,0:T(8,128)(2,1)S(1)}) custom-call(s32[4,25]{1,0:T(4,128)S(1)} %get-tuple-element.65.table, bf16[128,1024]{1,0:T(8,128)(2,1)S(1)} %get-tuple-element.51.refs_0_.q_ref, ...), custom_call_target="tpu_custom_call" | custom-call | flops 3221225472 | bytes 3670016 | tf_op jit(solution)/shard_map/pallas_call | solution.py:131
  154.3 3.5 %collective-permute-start.13 = (bf16[128,1152]{1,0:T(8,128)(2,1)}, bf16[128,1152]{1,0:T(8,128)(2,1)}, u32[]{:S(2)}, u32[]{:S(2)}) collective-permute-start(bf16[128,1152]{1,0:T(8,128)(2,1)} %get-tuple-element.28), channel_id=1, source_target_pairs={{0,4},{4,0},{1,5},{5,1},{2,6},{6,2},{3,7},{7,3},{8,12},{12,8},{9,1... | collective-permute-start | bytes 884744 | tf_op jit(solution)/shard_map/ppermute | solution.py:20
  158.5 4.2 %collective-permute-start.10 = (bf16[128,1152]{1,0:T(8,128)(2,1)S(1)}, bf16[128,1152]{1,0:T(8,128)(2,1)}, u32[]{:S(2)}, u32[]{:S(2)}) collective-permute-start(bf16[128,1152]{1,0:T(8,128)(2,1)S(1)} %shard_map.85), channel_id=1, source_target_pairs={{0,16},{8,24},{16,0},{24,8},{1,17},{9,25},{17,1},{25,9},{2,18},{10... | collective-permute-start | bytes 884744 | tf_op jit(solution)/shard_map/ppermute | solution.py:20
  163.8 1.4 collective-permute-start.12
  166.8 2.3 shard_map.95
  169.0 2.5 collective-permute-start.41
  171.6 4.4 %collective-permute-start.40 = (bf16[128,1024]{1,0:T(8,128)(2,1)S(1)}, bf16[128,1024]{1,0:T(8,128)(2,1)S(1)}, u32[]{:S(2)}, u32[]{:S(2)}) collective-permute-start(bf16[128,1024]{1,0:T(8,128)(2,1)S(1)} %shard_map.95), channel_id=1, source_target_pairs={{0,16},{8,24},{16,0},{24,8},{1,17},{9,25},{17,1},{25,9},{2,18},{10... | collective-permute-start | bytes 786440 | tf_op jit(solution)/shard_map/ppermute | solution.py:20
  176.0 13.6 %collective-permute-done.10.refs_1_ = bf16[128,1152]{1,0:T(8,128)(2,1)} collective-permute-done((bf16[128,1152]{1,0:T(8,128)(2,1)S(1)}, bf16[128,1152]{1,0:T(8,128)(2,1)}, u32[]{:S(2)}, u32[]{:S(2)}) %collective-permute-start.10) | collective-permute-done | bytes 294944 | tf_op jit(solution)/shard_map/ppermute | solution.py:20
  190.3 2.2 shard_map.88
  193.4 9.9 %collective-permute-start.15 = (bf16[128,1024]{1,0:T(8,128)(2,1)S(1)}, bf16[128,1024]{1,0:T(8,128)(2,1)S(1)}, u32[]{:S(2)}, u32[]{:S(2)}) collective-permute-start(bf16[128,1024]{1,0:T(8,128)(2,1)S(1)} %shard_map.88), channel_id=1, source_target_pairs={{0,16},{8,24},{16,0},{24,8},{1,17},{9,25},{17,1},{25,9},{2,18},{10... | collective-permute-start | bytes 786440 | tf_op jit(solution)/shard_map/ppermute | solution.py:20
  203.4 7.0 %collective-permute-start.14 = (bf16[128,1024]{1,0:T(8,128)(2,1)S(1)}, bf16[128,1024]{1,0:T(8,128)(2,1)S(1)}, u32[]{:S(2)}, u32[]{:S(2)}) collective-permute-start(bf16[128,1024]{1,0:T(8,128)(2,1)S(1)} %shard_map.88), channel_id=1, source_target_pairs={{0,8},{8,0},{16,24},{24,16},{1,9},{9,1},{17,25},{25,17},{2,10},{10... | collective-permute-start | bytes 786440 | tf_op jit(solution)/shard_map/ppermute | solution.py:20
  210.3 5.2 %collective-permute-done.40 = bf16[128,1024]{1,0:T(8,128)(2,1)S(1)} collective-permute-done((bf16[128,1024]{1,0:T(8,128)(2,1)S(1)}, bf16[128,1024]{1,0:T(8,128)(2,1)S(1)}, u32[]{:S(2)}, u32[]{:S(2)}) %collective-permute-start.40) | collective-permute-done | bytes 262176 | tf_op jit(solution)/shard_map/ppermute | solution.py:20
  215.5 2.1 convolution_convert_fusion.2
  218.6 4.7 %collective-permute-done.15 = bf16[128,1024]{1,0:T(8,128)(2,1)S(1)} collective-permute-done((bf16[128,1024]{1,0:T(8,128)(2,1)S(1)}, bf16[128,1024]{1,0:T(8,128)(2,1)S(1)}, u32[]{:S(2)}, u32[]{:S(2)}) %collective-permute-start.15) | collective-permute-done | bytes 262176 | tf_op jit(solution)/shard_map/ppermute | solution.py:20
  225.9 2.1 fusion.2
  227.9 1.6 collective-permute-start.43
  229.5 2.5 fusion.11
  232.6 10.2 %collective-permute-done.43 = bf16[512,512]{1,0:T(8,128)(2,1)S(1)} collective-permute-done((bf16[512,512]{1,0:T(8,128)(2,1)S(1)}, bf16[512,512]{1,0:T(8,128)(2,1)S(1)}, u32[]{:S(2)}, u32[]{:S(2)}) %collective-permute-start.43) | collective-permute-done | bytes 524320 | tf_op jit(solution)/shard_map/ppermute | solution.py:20
  242.8 1.8 fusion.8
  244.9 4.3 %collective-permute-start.44 = (bf16[128,512]{1,0:T(8,128)(2,1)S(1)}, bf16[128,512]{1,0:T(8,128)(2,1)S(1)}, u32[]{:S(2)}, u32[]{:S(2)}) collective-permute-start(bf16[128,512]{1,0:T(8,128)(2,1)S(1)} %get-tuple-element.49), channel_id=1, source_target_pairs={{0,8},{8,0},{16,24},{24,16},{1,9},{9,1},{17,25},{25,17},{2,10},{10... | collective-permute-start | bytes 393224 | tf_op jit(solution)/shard_map/ppermute | solution.py:20
  249.1 3.7 %collective-permute-done.18 = bf16[512,512]{1,0:T(8,128)(2,1)S(1)} collective-permute-done((bf16[512,512]{1,0:T(8,128)(2,1)S(1)}, bf16[512,512]{1,0:T(8,128)(2,1)S(1)}, u32[]{:S(2)}, u32[]{:S(2)}) %collective-permute-start.18) | collective-permute-done | bytes 524320 | tf_op jit(solution)/shard_map/ppermute | solution.py:20
  252.8 1.8 fusion.17
  255.8 1.9 collective-permute-start.47
  258.6 3.5 %collective-permute-start.19 = (bf16[128,512]{1,0:T(8,128)(2,1)S(1)}, bf16[128,512]{1,0:T(8,128)(2,1)S(1)}, u32[]{:S(2)}, u32[]{:S(2)}) collective-permute-start(bf16[128,512]{1,0:T(8,128)(2,1)S(1)} %get-tuple-element.57), channel_id=1, source_target_pairs={{0,8},{8,0},{16,24},{24,16},{1,9},{9,1},{17,25},{25,17},{2,10},{10... | collective-permute-start | bytes 393224 | tf_op jit(solution)/shard_map/ppermute | solution.py:20
  262.1 3.9 %collective-permute-done.21 = bf16[128,512]{1,0:T(8,128)(2,1)S(1)} collective-permute-done((bf16[128,512]{1,0:T(8,128)(2,1)S(1)}, bf16[128,512]{1,0:T(8,128)(2,1)S(1)}, u32[]{:S(2)}, u32[]{:S(2)}) %collective-permute-start.21) | collective-permute-done | bytes 131104 | tf_op jit(solution)/shard_map/ppermute | solution.py:20
  266.0 3.4 %collective-permute-done.20 = bf16[128,512]{1,0:T(8,128)(2,1)S(1)} collective-permute-done((bf16[128,512]{1,0:T(8,128)(2,1)S(1)}, bf16[128,512]{1,0:T(8,128)(2,1)S(1)}, u32[]{:S(2)}, u32[]{:S(2)}) %collective-permute-start.20) | collective-permute-done | bytes 131104 | tf_op jit(solution)/shard_map/ppermute | solution.py:20
  271.1 11.6 %collective-permute-done.22 = bf16[1,4,128,512]{3,2,1,0:T(8,128)(2,1)S(1)} collective-permute-done((bf16[1,4,128,512]{3,2,1,0:T(8,128)(2,1)S(1)}, bf16[1,4,128,512]{3,2,1,0:T(8,128)(2,1)S(1)}, u32[]{:S(2)}, u32[]{:S(2)}) %collective-permute-start.22) | collective-permute-done | bytes 524320 | tf_op jit(solution)/shard_map/ppermute | solution.py:20
  285.3 2.1 shard_map.96.refs_4_
  287.5 2.1 shard_map.97
  (169 shorter events, 31.3 us)
Async XLA Ops:
  1.2 44.6 %collective-permute-start.27 = (bf16[128,1024]{1,0:T(8,128)(2,1)S(1)}, bf16[128,1024]{1,0:T(8,128)(2,1)}, u32[]{:S(2)}, u32[]{:S(2)}) collective-permute-start(bf16[128,1024]{1,0:T(8,128)(2,1)S(1)} %get-tuple-element.50.refs_0_.q_ref), channel_id=1, source_target_pairs={{0,4},{4,0},{1,5},{5,1},{2,6},{6,2},{3,7},{7,3},{8,12},{12,8},{9,1... | collective-permute-start | bytes 786440 | tf_op jit(solution)/shard_map/ppermute | solution.py:20
  4.2 48.6 %collective-permute-start.26 = (bf16[128,1024]{1,0:T(8,128)(2,1)S(1)}, bf16[128,1024]{1,0:T(8,128)(2,1)S(1)}, u32[]{:S(2)}, u32[]{:S(2)}) collective-permute-start(bf16[128,1024]{1,0:T(8,128)(2,1)S(1)} %get-tuple-element.50.refs_0_.q_ref), channel_id=1, source_target_pairs={{0,24},{8,16},{16,8},{24,0},{1,25},{9,17},{17,9},{25,1},{2,26},{10... | collective-permute-start | bytes 786440 | tf_op jit(solution)/shard_map/ppermute | solution.py:20
  7.8 45.5 %collective-permute-start.25 = (bf16[128,1024]{1,0:T(8,128)(2,1)S(1)}, bf16[128,1024]{1,0:T(8,128)(2,1)}, u32[]{:S(2)}, u32[]{:S(2)}) collective-permute-start(bf16[128,1024]{1,0:T(8,128)(2,1)S(1)} %get-tuple-element.50.refs_0_.q_ref), channel_id=1, source_target_pairs={{0,16},{8,24},{16,0},{24,8},{1,17},{9,25},{17,1},{25,9},{2,18},{10... | collective-permute-start | bytes 786440 | tf_op jit(solution)/shard_map/ppermute | solution.py:20
  7.8 46.9 %collective-permute-start.24 = (bf16[128,1024]{1,0:T(8,128)(2,1)S(1)}, bf16[128,1024]{1,0:T(8,128)(2,1)}, u32[]{:S(2)}, u32[]{:S(2)}) collective-permute-start(bf16[128,1024]{1,0:T(8,128)(2,1)S(1)} %get-tuple-element.50.refs_0_.q_ref), channel_id=1, source_target_pairs={{0,8},{8,0},{16,24},{24,16},{1,9},{9,1},{17,25},{25,17},{2,10},{10... | collective-permute-start | bytes 786440 | tf_op jit(solution)/shard_map/ppermute | solution.py:20
  8.6 47.5 %collective-permute-start.2 = (bf16[128,1024]{1,0:T(8,128)(2,1)S(1)}, bf16[128,1024]{1,0:T(8,128)(2,1)S(1)}, u32[]{:S(2)}, u32[]{:S(2)}) collective-permute-start(bf16[128,1024]{1,0:T(8,128)(2,1)S(1)} %get-tuple-element.51.refs_0_.q_ref), channel_id=1, source_target_pairs={{0,24},{8,16},{16,8},{24,0},{1,25},{9,17},{17,9},{25,1},{2,26},{10... | collective-permute-start | bytes 786440 | tf_op jit(solution)/shard_map/ppermute | solution.py:20
  45.9 15.6 %collective-permute-start.1 = (bf16[128,1024]{1,0:T(8,128)(2,1)S(1)}, bf16[128,1024]{1,0:T(8,128)(2,1)}, u32[]{:S(2)}, u32[]{:S(2)}) collective-permute-start(bf16[128,1024]{1,0:T(8,128)(2,1)S(1)} %get-tuple-element.51.refs_0_.q_ref), channel_id=1, source_target_pairs={{0,16},{8,24},{16,0},{24,8},{1,17},{9,25},{17,1},{25,9},{2,18},{10... | collective-permute-start | bytes 786440 | tf_op jit(solution)/shard_map/ppermute | solution.py:20
  52.8 8.9 %collective-permute-start = (bf16[128,1024]{1,0:T(8,128)(2,1)S(1)}, bf16[128,1024]{1,0:T(8,128)(2,1)}, u32[]{:S(2)}, u32[]{:S(2)}) collective-permute-start(bf16[128,1024]{1,0:T(8,128)(2,1)S(1)} %get-tuple-element.51.refs_0_.q_ref), channel_id=1, source_target_pairs={{0,8},{8,0},{16,24},{24,16},{1,9},{9,1},{17,25},{25,17},{2,10},{10... | collective-permute-start | bytes 786440 | tf_op jit(solution)/shard_map/ppermute | solution.py:20
  53.4 12.1 %collective-permute-start.30 = (bf16[128,1024]{1,0:T(8,128)(2,1)S(1)}, bf16[128,1024]{1,0:T(8,128)(2,1)}, u32[]{:S(2)}, u32[]{:S(2)}) collective-permute-start(bf16[128,1024]{1,0:T(8,128)(2,1)S(1)} %collective-permute-done.26.refs_3_), channel_id=1, source_target_pairs={{0,4},{4,0},{1,5},{5,1},{2,6},{6,2},{3,7},{7,3},{8,12},{12,8},{9,1... | collective-permute-start | bytes 786440 | tf_op jit(solution)/shard_map/ppermute | solution.py:20
  54.7 13.6 %collective-permute-start.29 = (bf16[128,1024]{1,0:T(8,128)(2,1)}, bf16[128,1024]{1,0:T(8,128)(2,1)}, u32[]{:S(2)}, u32[]{:S(2)}) collective-permute-start(bf16[128,1024]{1,0:T(8,128)(2,1)} %collective-permute-done.25.refs_2_), channel_id=1, source_target_pairs={{0,4},{4,0},{1,5},{5,1},{2,6},{6,2},{3,7},{7,3},{8,12},{12,8},{9,1... | collective-permute-start | bytes 786440 | tf_op jit(solution)/shard_map/ppermute | solution.py:20
  56.1 17.9 %collective-permute-start.28 = (bf16[128,1024]{1,0:T(8,128)(2,1)}, bf16[128,1024]{1,0:T(8,128)(2,1)}, u32[]{:S(2)}, u32[]{:S(2)}) collective-permute-start(bf16[128,1024]{1,0:T(8,128)(2,1)} %collective-permute-done.24.refs_1_), channel_id=1, source_target_pairs={{0,4},{4,0},{1,5},{5,1},{2,6},{6,2},{3,7},{7,3},{8,12},{12,8},{9,1... | collective-permute-start | bytes 786440 | tf_op jit(solution)/shard_map/ppermute | solution.py:20
  61.5 27.1 %collective-permute-start.3 = (bf16[128,1024]{1,0:T(8,128)(2,1)S(1)}, bf16[128,1024]{1,0:T(8,128)(2,1)S(1)}, u32[]{:S(2)}, u32[]{:S(2)}) collective-permute-start(bf16[128,1024]{1,0:T(8,128)(2,1)S(1)} %get-tuple-element.51.refs_0_.q_ref), channel_id=1, source_target_pairs={{0,4},{4,0},{1,5},{5,1},{2,6},{6,2},{3,7},{7,3},{8,12},{12,8},{9,1... | collective-permute-start | bytes 786440 | tf_op jit(solution)/shard_map/ppermute | solution.py:20
  61.7 76.4 %collective-permute-start.38 = (bf16[128,256]{1,0:T(8,128)(2,1)S(1)}, bf16[128,256]{1,0:T(8,128)(2,1)S(1)}, u32[]{:S(2)}, u32[]{:S(2)}) collective-permute-start(bf16[128,256]{1,0:T(8,128)(2,1)S(1)} %pad_maximum_fusion.8), channel_id=1, source_target_pairs={{0,4},{4,8},{8,12},{12,16},{16,20},{20,24},{24,28},{1,5},{5,9},{9,... | collective-permute-start | bytes 196616 | tf_op jit(solution)/shard_map/ppermute | solution.py:279
  65.4 29.0 %collective-permute-start.6 = (bf16[128,1024]{1,0:T(8,128)(2,1)S(1)}, bf16[128,1024]{1,0:T(8,128)(2,1)S(1)}, u32[]{:S(2)}, u32[]{:S(2)}) collective-permute-start(bf16[128,1024]{1,0:T(8,128)(2,1)S(1)} %collective-permute-done.2.refs_3_), channel_id=1, source_target_pairs={{0,4},{4,0},{1,5},{5,1},{2,6},{6,2},{3,7},{7,3},{8,12},{12,8},{9,1... | collective-permute-start | bytes 786440 | tf_op jit(solution)/shard_map/ppermute | solution.py:20
  68.3 26.1 %collective-permute-start.5 = (bf16[128,1024]{1,0:T(8,128)(2,1)}, bf16[128,1024]{1,0:T(8,128)(2,1)S(1)}, u32[]{:S(2)}, u32[]{:S(2)}) collective-permute-start(bf16[128,1024]{1,0:T(8,128)(2,1)} %collective-permute-done.1.refs_2_), channel_id=1, source_target_pairs={{0,4},{4,0},{1,5},{5,1},{2,6},{6,2},{3,7},{7,3},{8,12},{12,8},{9,1... | collective-permute-start | bytes 786440 | tf_op jit(solution)/shard_map/ppermute | solution.py:20
  74.0 20.5 %collective-permute-start.4 = (bf16[128,1024]{1,0:T(8,128)(2,1)}, bf16[128,1024]{1,0:T(8,128)(2,1)S(1)}, u32[]{:S(2)}, u32[]{:S(2)}) collective-permute-start(bf16[128,1024]{1,0:T(8,128)(2,1)} %collective-permute-done.refs_1_), channel_id=1, source_target_pairs={{0,4},{4,0},{1,5},{5,1},{2,6},{6,2},{3,7},{7,3},{8,12},{12,8},{9,1... | collective-permute-start | bytes 786440 | tf_op jit(solution)/shard_map/ppermute | solution.py:20
  88.6 25.5 %collective-permute-start.35 = (bf16[128,1152]{1,0:T(8,128)(2,1)S(1)}, bf16[128,1152]{1,0:T(8,128)(2,1)S(1)}, u32[]{:S(2)}, u32[]{:S(2)}) collective-permute-start(bf16[128,1152]{1,0:T(8,128)(2,1)S(1)} %get-tuple-element.34), channel_id=1, source_target_pairs={{0,4},{4,0},{1,5},{5,1},{2,6},{6,2},{3,7},{7,3},{8,12},{12,8},{9,1... | collective-permute-start | bytes 884744 | tf_op jit(solution)/shard_map/ppermute | solution.py:20
  107.7 30.5 %collective-permute-start.7 = (bf16[128,1152]{1,0:T(8,128)(2,1)S(1)}, bf16[128,1152]{1,0:T(8,128)(2,1)S(1)}, u32[]{:S(2)}, u32[]{:S(2)}) collective-permute-start(bf16[128,1152]{1,0:T(8,128)(2,1)S(1)} %get-tuple-element.22), channel_id=1, source_target_pairs={{0,4},{4,0},{1,5},{5,1},{2,6},{6,2},{3,7},{7,3},{8,12},{12,8},{9,1... | collective-permute-start | bytes 884744 | tf_op jit(solution)/shard_map/ppermute | solution.py:20
  112.1 26.2 %collective-permute-start.9 = (bf16[128,1152]{1,0:T(8,128)(2,1)S(1)}, bf16[128,1152]{1,0:T(8,128)(2,1)S(1)}, u32[]{:S(2)}, u32[]{:S(2)}) collective-permute-start(bf16[128,1152]{1,0:T(8,128)(2,1)S(1)} %get-tuple-element.24), channel_id=1, source_target_pairs={{0,4},{4,0},{1,5},{5,1},{2,6},{6,2},{3,7},{7,3},{8,12},{12,8},{9,1... | collective-permute-start | bytes 884744 | tf_op jit(solution)/shard_map/ppermute | solution.py:20
  112.2 20.5 %collective-permute-start.31 = (bf16[128,1152]{1,0:T(8,128)(2,1)S(1)}, bf16[128,1152]{1,0:T(8,128)(2,1)S(1)}, u32[]{:S(2)}, u32[]{:S(2)}) collective-permute-start(bf16[128,1152]{1,0:T(8,128)(2,1)S(1)} %get-tuple-element.30), channel_id=1, source_target_pairs={{0,4},{4,0},{1,5},{5,1},{2,6},{6,2},{3,7},{7,3},{8,12},{12,8},{9,1... | collective-permute-start | bytes 884744 | tf_op jit(solution)/shard_map/ppermute | solution.py:20
  114.1 21.8 %collective-permute-start.33 = (bf16[128,1152]{1,0:T(8,128)(2,1)S(1)}, bf16[128,1152]{1,0:T(8,128)(2,1)S(1)}, u32[]{:S(2)}, u32[]{:S(2)}) collective-permute-start(bf16[128,1152]{1,0:T(8,128)(2,1)S(1)} %get-tuple-element.32), channel_id=1, source_target_pairs={{0,4},{4,0},{1,5},{5,1},{2,6},{6,2},{3,7},{7,3},{8,12},{12,8},{9,1... | collective-permute-start | bytes 884744 | tf_op jit(solution)/shard_map/ppermute | solution.py:20
  132.7 21.6 %collective-permute-start.11 = (bf16[128,1152]{1,0:T(8,128)(2,1)S(1)}, bf16[128,1152]{1,0:T(8,128)(2,1)S(1)}, u32[]{:S(2)}, u32[]{:S(2)}) collective-permute-start(bf16[128,1152]{1,0:T(8,128)(2,1)S(1)} %get-tuple-element.26), channel_id=1, source_target_pairs={{0,4},{4,0},{1,5},{5,1},{2,6},{6,2},{3,7},{7,3},{8,12},{12,8},{9,1... | collective-permute-start | bytes 884744 | tf_op jit(solution)/shard_map/ppermute | solution.py:20
  135.9 21.9 %collective-permute-start.37 = (bf16[128,1152]{1,0:T(8,128)(2,1)S(1)}, bf16[128,1152]{1,0:T(8,128)(2,1)S(1)}, u32[]{:S(2)}, u32[]{:S(2)}) collective-permute-start(bf16[128,1152]{1,0:T(8,128)(2,1)S(1)} %get-tuple-element.36), channel_id=1, source_target_pairs={{0,4},{4,0},{1,5},{5,1},{2,6},{6,2},{3,7},{7,3},{8,12},{12,8},{9,1... | collective-permute-start | bytes 884744 | tf_op jit(solution)/shard_map/ppermute | solution.py:20
  138.1 25.6 %collective-permute-start.34 = (bf16[128,1152]{1,0:T(8,128)(2,1)S(1)}, bf16[128,1152]{1,0:T(8,128)(2,1)}, u32[]{:S(2)}, u32[]{:S(2)}) collective-permute-start(bf16[128,1152]{1,0:T(8,128)(2,1)S(1)} %shard_map.92), channel_id=1, source_target_pairs={{0,16},{8,24},{16,0},{24,8},{1,17},{9,25},{17,1},{25,9},{2,18},{10... | collective-permute-start | bytes 884744 | tf_op jit(solution)/shard_map/ppermute | solution.py:20
  138.2 25.6 %collective-permute-start.32 = (bf16[128,1152]{1,0:T(8,128)(2,1)S(1)}, bf16[128,1152]{1,0:T(8,128)(2,1)}, u32[]{:S(2)}, u32[]{:S(2)}) collective-permute-start(bf16[128,1152]{1,0:T(8,128)(2,1)S(1)} %shard_map.91), channel_id=1, source_target_pairs={{0,8},{8,0},{16,24},{24,16},{1,9},{9,1},{17,25},{25,17},{2,10},{10... | collective-permute-start | bytes 884744 | tf_op jit(solution)/shard_map/ppermute | solution.py:20
  138.3 28.5 %collective-permute-start.36 = (bf16[128,1152]{1,0:T(8,128)(2,1)S(1)}, bf16[128,1152]{1,0:T(8,128)(2,1)}, u32[]{:S(2)}, u32[]{:S(2)}) collective-permute-start(bf16[128,1152]{1,0:T(8,128)(2,1)S(1)} %shard_map.93), channel_id=1, source_target_pairs={{0,24},{8,16},{16,8},{24,0},{1,25},{9,17},{17,9},{25,1},{2,26},{10... | collective-permute-start | bytes 884744 | tf_op jit(solution)/shard_map/ppermute | solution.py:20
  154.3 17.3 %collective-permute-start.13 = (bf16[128,1152]{1,0:T(8,128)(2,1)}, bf16[128,1152]{1,0:T(8,128)(2,1)}, u32[]{:S(2)}, u32[]{:S(2)}) collective-permute-start(bf16[128,1152]{1,0:T(8,128)(2,1)} %get-tuple-element.28), channel_id=1, source_target_pairs={{0,4},{4,0},{1,5},{5,1},{2,6},{6,2},{3,7},{7,3},{8,12},{12,8},{9,1... | collective-permute-start | bytes 884744 | tf_op jit(solution)/shard_map/ppermute | solution.py:20
  158.5 31.0 %collective-permute-start.10 = (bf16[128,1152]{1,0:T(8,128)(2,1)S(1)}, bf16[128,1152]{1,0:T(8,128)(2,1)}, u32[]{:S(2)}, u32[]{:S(2)}) collective-permute-start(bf16[128,1152]{1,0:T(8,128)(2,1)S(1)} %shard_map.85), channel_id=1, source_target_pairs={{0,16},{8,24},{16,0},{24,8},{1,17},{9,25},{17,1},{25,9},{2,18},{10... | collective-permute-start | bytes 884744 | tf_op jit(solution)/shard_map/ppermute | solution.py:20
  163.7 26.6 %collective-permute-start.8 = (bf16[128,1152]{1,0:T(8,128)(2,1)S(1)}, bf16[128,1152]{1,0:T(8,128)(2,1)S(1)}, u32[]{:S(2)}, u32[]{:S(2)}) collective-permute-start(bf16[128,1152]{1,0:T(8,128)(2,1)S(1)} %shard_map.84), channel_id=1, source_target_pairs={{0,8},{8,0},{16,24},{24,16},{1,9},{9,1},{17,25},{25,17},{2,10},{10... | collective-permute-start | bytes 884744 | tf_op jit(solution)/shard_map/ppermute | solution.py:20
  163.8 26.5 %collective-permute-start.12 = (bf16[128,1152]{1,0:T(8,128)(2,1)S(1)}, bf16[128,1152]{1,0:T(8,128)(2,1)S(1)}, u32[]{:S(2)}, u32[]{:S(2)}) collective-permute-start(bf16[128,1152]{1,0:T(8,128)(2,1)S(1)} %shard_map.86), channel_id=1, source_target_pairs={{0,24},{8,16},{16,8},{24,0},{1,25},{9,17},{17,9},{25,1},{2,26},{10... | collective-permute-start | bytes 884744 | tf_op jit(solution)/shard_map/ppermute | solution.py:20
  169.0 34.3 %collective-permute-start.41 = (bf16[128,1024]{1,0:T(8,128)(2,1)S(1)}, bf16[128,1024]{1,0:T(8,128)(2,1)S(1)}, u32[]{:S(2)}, u32[]{:S(2)}) collective-permute-start(bf16[128,1024]{1,0:T(8,128)(2,1)S(1)} %shard_map.95), channel_id=1, source_target_pairs={{0,24},{8,16},{16,8},{24,0},{1,25},{9,17},{17,9},{25,1},{2,26},{10... | collective-permute-start | bytes 786440 | tf_op jit(solution)/shard_map/ppermute | solution.py:20
  171.6 43.9 %collective-permute-start.40 = (bf16[128,1024]{1,0:T(8,128)(2,1)S(1)}, bf16[128,1024]{1,0:T(8,128)(2,1)S(1)}, u32[]{:S(2)}, u32[]{:S(2)}) collective-permute-start(bf16[128,1024]{1,0:T(8,128)(2,1)S(1)} %shard_map.95), channel_id=1, source_target_pairs={{0,16},{8,24},{16,0},{24,8},{1,17},{9,25},{17,1},{25,9},{2,18},{10... | collective-permute-start | bytes 786440 | tf_op jit(solution)/shard_map/ppermute | solution.py:20
  189.5 26.0 %collective-permute-start.39 = (bf16[128,1024]{1,0:T(8,128)(2,1)S(1)}, bf16[128,1024]{1,0:T(8,128)(2,1)S(1)}, u32[]{:S(2)}, u32[]{:S(2)}) collective-permute-start(bf16[128,1024]{1,0:T(8,128)(2,1)S(1)} %shard_map.95), channel_id=1, source_target_pairs={{0,8},{8,0},{16,24},{24,16},{1,9},{9,1},{17,25},{25,17},{2,10},{10... | collective-permute-start | bytes 786440 | tf_op jit(solution)/shard_map/ppermute | solution.py:20
  192.5 26.1 %collective-permute-start.16 = (bf16[128,1024]{1,0:T(8,128)(2,1)S(1)}, bf16[128,1024]{1,0:T(8,128)(2,1)S(1)}, u32[]{:S(2)}, u32[]{:S(2)}) collective-permute-start(bf16[128,1024]{1,0:T(8,128)(2,1)S(1)} %shard_map.88), channel_id=1, source_target_pairs={{0,24},{8,16},{16,8},{24,0},{1,25},{9,17},{17,9},{25,1},{2,26},{10... | collective-permute-start | bytes 786440 | tf_op jit(solution)/shard_map/ppermute | solution.py:20
  193.4 29.9 %collective-permute-start.15 = (bf16[128,1024]{1,0:T(8,128)(2,1)S(1)}, bf16[128,1024]{1,0:T(8,128)(2,1)S(1)}, u32[]{:S(2)}, u32[]{:S(2)}) collective-permute-start(bf16[128,1024]{1,0:T(8,128)(2,1)S(1)} %shard_map.88), channel_id=1, source_target_pairs={{0,16},{8,24},{16,0},{24,8},{1,17},{9,25},{17,1},{25,9},{2,18},{10... | collective-permute-start | bytes 786440 | tf_op jit(solution)/shard_map/ppermute | solution.py:20
  203.4 20.0 %collective-permute-start.14 = (bf16[128,1024]{1,0:T(8,128)(2,1)S(1)}, bf16[128,1024]{1,0:T(8,128)(2,1)S(1)}, u32[]{:S(2)}, u32[]{:S(2)}) collective-permute-start(bf16[128,1024]{1,0:T(8,128)(2,1)S(1)} %shard_map.88), channel_id=1, source_target_pairs={{0,8},{8,0},{16,24},{24,16},{1,9},{9,1},{17,25},{25,17},{2,10},{10... | collective-permute-start | bytes 786440 | tf_op jit(solution)/shard_map/ppermute | solution.py:20
  218.5 6.5 %collective-permute-start.42 = (bf16[512,1024]{1,0:T(8,128)(2,1)S(1)}, bf16[512,1024]{1,0:T(8,128)(2,1)}, u32[]{:S(2)}, u32[]{:S(2)}) collective-permute-start(bf16[512,1024]{1,0:T(8,128)(2,1)S(1)} %pad_maximum_fusion.4), channel_id=1, source_target_pairs={{0,1},{1,0},{2,3},{3,2},{4,5},{5,4},{6,7},{7,6},{8,9},{9,8},{10,11... | collective-permute-start | bytes 3145736 | tf_op jit(solution)/shard_map/ppermute | solution.py:20
  225.0 4.5 %collective-permute-start.17 = (bf16[512,1024]{1,0:T(8,128)(2,1)S(1)}, bf16[512,1024]{1,0:T(8,128)(2,1)}, u32[]{:S(2)}, u32[]{:S(2)}) collective-permute-start(bf16[512,1024]{1,0:T(8,128)(2,1)S(1)} %pad_maximum_fusion.1), channel_id=1, source_target_pairs={{0,1},{1,0},{2,3},{3,2},{4,5},{5,4},{6,7},{7,6},{8,9},{9,8},{10,11... | collective-permute-start | bytes 3145736 | tf_op jit(solution)/shard_map/ppermute | solution.py:20
  227.9 14.9 %collective-permute-start.43 = (bf16[512,512]{1,0:T(8,128)(2,1)S(1)}, bf16[512,512]{1,0:T(8,128)(2,1)S(1)}, u32[]{:S(2)}, u32[]{:S(2)}) collective-permute-start(bf16[512,512]{1,0:T(8,128)(2,1)S(1)} %fusion.2), channel_id=1, source_target_pairs={{0,2},{1,3},{2,0},{3,1},{4,6},{5,7},{6,4},{7,5},{8,10},{9,11},{10,... | collective-permute-start | bytes 1572872 | tf_op jit(solution)/shard_map/ppermute | solution.py:20
  232.0 20.8 %collective-permute-start.18 = (bf16[512,512]{1,0:T(8,128)(2,1)S(1)}, bf16[512,512]{1,0:T(8,128)(2,1)S(1)}, u32[]{:S(2)}, u32[]{:S(2)}) collective-permute-start(bf16[512,512]{1,0:T(8,128)(2,1)S(1)} %fusion.11), channel_id=1, source_target_pairs={{0,2},{1,3},{2,0},{3,1},{4,6},{5,7},{6,4},{7,5},{8,10},{9,11},{10,... | collective-permute-start | bytes 1572872 | tf_op jit(solution)/shard_map/ppermute | solution.py:20
  244.7 9.9 %collective-permute-start.46 = (bf16[128,512]{1,0:T(8,128)(2,1)S(1)}, bf16[128,512]{1,0:T(8,128)(2,1)S(1)}, u32[]{:S(2)}, u32[]{:S(2)}) collective-permute-start(bf16[128,512]{1,0:T(8,128)(2,1)S(1)} %get-tuple-element.47), channel_id=1, source_target_pairs={{0,24},{8,16},{16,8},{24,0},{1,25},{9,17},{17,9},{25,1},{2,26},{10... | collective-permute-start | bytes 393224 | tf_op jit(solution)/shard_map/ppermute | solution.py:20
  244.8 10.9 %collective-permute-start.45 = (bf16[128,512]{1,0:T(8,128)(2,1)S(1)}, bf16[128,512]{1,0:T(8,128)(2,1)S(1)}, u32[]{:S(2)}, u32[]{:S(2)}) collective-permute-start(bf16[128,512]{1,0:T(8,128)(2,1)S(1)} %get-tuple-element.48), channel_id=1, source_target_pairs={{0,16},{8,24},{16,0},{24,8},{1,17},{9,25},{17,1},{25,9},{2,18},{10... | collective-permute-start | bytes 393224 | tf_op jit(solution)/shard_map/ppermute | solution.py:20
  244.9 10.8 %collective-permute-start.44 = (bf16[128,512]{1,0:T(8,128)(2,1)S(1)}, bf16[128,512]{1,0:T(8,128)(2,1)S(1)}, u32[]{:S(2)}, u32[]{:S(2)}) collective-permute-start(bf16[128,512]{1,0:T(8,128)(2,1)S(1)} %get-tuple-element.49), channel_id=1, source_target_pairs={{0,8},{8,0},{16,24},{24,16},{1,9},{9,1},{17,25},{25,17},{2,10},{10... | collective-permute-start | bytes 393224 | tf_op jit(solution)/shard_map/ppermute | solution.py:20
  255.8 14.3 %collective-permute-start.47 = (bf16[1,4,128,512]{3,2,1,0:T(8,128)(2,1)S(1)}, bf16[1,4,128,512]{3,2,1,0:T(8,128)(2,1)S(1)}, u32[]{:S(2)}, u32[]{:S(2)}) collective-permute-start(bf16[1,4,128,512]{3,2,1,0:T(8,128)(2,1)S(1)} %get-tuple-element.44), channel_id=1, source_target_pairs={{0,2},{1,3},{2,0},{3,1},{4,6},{5,7},{6,4},{7,5},{8,10},{9,11},{10,... | collective-permute-start | bytes 1572872 | tf_op jit(solution)/shard_map/ppermute | solution.py:20
  257.7 8.3 %collective-permute-start.21 = (bf16[128,512]{1,0:T(8,128)(2,1)S(1)}, bf16[128,512]{1,0:T(8,128)(2,1)S(1)}, u32[]{:S(2)}, u32[]{:S(2)}) collective-permute-start(bf16[128,512]{1,0:T(8,128)(2,1)S(1)} %get-tuple-element.55), channel_id=1, source_target_pairs={{0,24},{8,16},{16,8},{24,0},{1,25},{9,17},{17,9},{25,1},{2,26},{10... | collective-permute-start | bytes 393224 | tf_op jit(solution)/shard_map/ppermute | solution.py:20
  258.6 10.8 %collective-permute-start.20 = (bf16[128,512]{1,0:T(8,128)(2,1)S(1)}, bf16[128,512]{1,0:T(8,128)(2,1)S(1)}, u32[]{:S(2)}, u32[]{:S(2)}) collective-permute-start(bf16[128,512]{1,0:T(8,128)(2,1)S(1)} %get-tuple-element.56), channel_id=1, source_target_pairs={{0,16},{8,24},{16,0},{24,8},{1,17},{9,25},{17,1},{25,9},{2,18},{10... | collective-permute-start | bytes 393224 | tf_op jit(solution)/shard_map/ppermute | solution.py:20
  258.6 10.8 %collective-permute-start.19 = (bf16[128,512]{1,0:T(8,128)(2,1)S(1)}, bf16[128,512]{1,0:T(8,128)(2,1)S(1)}, u32[]{:S(2)}, u32[]{:S(2)}) collective-permute-start(bf16[128,512]{1,0:T(8,128)(2,1)S(1)} %get-tuple-element.57), channel_id=1, source_target_pairs={{0,8},{8,0},{16,24},{24,16},{1,9},{9,1},{17,25},{25,17},{2,10},{10... | collective-permute-start | bytes 393224 | tf_op jit(solution)/shard_map/ppermute | solution.py:20
  269.5 13.3 %collective-permute-start.22 = (bf16[1,4,128,512]{3,2,1,0:T(8,128)(2,1)S(1)}, bf16[1,4,128,512]{3,2,1,0:T(8,128)(2,1)S(1)}, u32[]{:S(2)}, u32[]{:S(2)}) collective-permute-start(bf16[1,4,128,512]{3,2,1,0:T(8,128)(2,1)S(1)} %get-tuple-element.52), channel_id=1, source_target_pairs={{0,2},{1,3},{2,0},{3,1},{4,6},{5,7},{6,4},{7,5},{8,10},{9,11},{10,... | collective-permute-start | bytes 1572872 | tf_op jit(solution)/shard_map/ppermute | solution.py:20
  271.1 12.9 %collective-permute-start.48 = (bf16[2,4,128,512]{3,2,1,0:T(8,128)(2,1)}, bf16[2,4,128,512]{3,2,1,0:T(8,128)(2,1)}, u32[]{:S(2)}, u32[]{:S(2)}) collective-permute-start(bf16[2,4,128,512]{3,2,1,0:T(8,128)(2,1)} %pad_maximum_fusion.5), channel_id=1, source_target_pairs={{0,1},{1,0},{2,3},{3,2},{4,5},{5,4},{6,7},{7,6},{8,9},{9,8},{10,11... | collective-permute-start | bytes 3145736 | tf_op jit(solution)/shard_map/ppermute | solution.py:20
  (31 other events, 576.5 us)
